TPU v7x, 32 devices: a whole 2x2x4 slice. The times are simulated.
32 devices in a mesh: dp: 8 (over z, core), tp: 4 (over y, x).
Axes of the slice: x: 2, y: 2, z: 4, core: 2. Of those that a mesh axis runs over, the one named last changes fastest.
Arguments:
- tokens: bfloat16 [4096, 2048], P(('dp', 'tp')), may hold values from -6 to 6
- upstream: bfloat16 [4096, 2048], P(('dp', 'tp')), may hold values from -6 to 6
- segment_ids: int32 [4096], P('dp'), may hold values from 0 to 11, as said below
- positions: int32 [4096], P('dp'), may hold values from 0 to 511, as said below
- norm_gain: float32 [2048], replicated, may hold values from 0.5 to 1.5
- norm_bias: float32 [2048], replicated, may hold values from -3 to 3
- qkv_weight: bfloat16 [2048, 3, 2048], P(None, None, 'tp'), may hold values from -0.125 to 0.125
- qkv_bias: bfloat16 [3, 2048], P(None, 'tp'), may hold values from -3 to 3
- dense_weight: bfloat16 [2048, 2048], P('tp'), may hold values from -0.5 to 0.5
- up_weight: bfloat16 [2048, 8192], P(None, 'tp'), may hold values from -0.125 to 0.125
- up_bias: bfloat16 [8192], P('tp'), may hold values from -3 to 3
- down_weight: bfloat16 [8192, 2048], P('tp'), may hold values from -0.125 to 0.125
- out_bias: float32 [2048], replicated, may hold values from -3 to 3
Outputs:
- mixed: bfloat16 [4096, 2048], P(('dp', 'tp'))
- input_grad: float32 [4096, 2048], P(('dp', 'tp'))
- norm_gain_grad: float32 [2048], replicated
- norm_bias_grad: float32 [2048], replicated
- qkv_weight_grad: float32 [2048, 3, 2048], P(None, None, 'tp')
- qkv_bias_grad: float32 [3, 2048], P(None, 'tp')
- dense_weight_grad: float32 [2048, 2048], P('tp')
- up_weight_grad: float32 [2048, 8192], P(None, 'tp')
- up_bias_grad: float32 [8192], P('tp')
- down_weight_grad: float32 [8192, 2048], P('tp')
- out_bias_grad: float32 [2048], replicated
Inputs may be any that keep to these rules, and one draw needn't show every extreme that they name: Each group of 512 tokens on one index of dp holds whole sequences with consecutive segment_ids, rising from group to group; in half of the groups every sequence has 512 tokens, in the other half 256. `positions`: every sequence holds each position from 0 to its length - 1 exactly once.
All inputs are finite; a program needn't handle non-finite values.
Results may differ from a plain program's by a relative error of at most 0.0074.
Values may be sent and summed in bfloat16 or wider, within the bound.
No kernel may reach another device: no remote copies, remote signals or barrier semaphores. Data moves between devices by JAX's collectives and lax.ppermute only.
A program may use at most 256 MiB of HBM per device.

v0:
```python
from functools import partial
import math

import jax
import jax.numpy as jnp
from jax import lax
from jax.sharding import PartitionSpec as P

HEAD_DIM = 64
ROT = 32


norm_epsilon = 1e-05
masked_score = -1e30


def layer_norm(values, gain, shift):
    averaged = jnp.mean(values, -1, keepdims=True)
    centred = values - averaged
    spread = jnp.mean(centred * centred, -1, keepdims=True)
    return centred * lax.rsqrt(spread + norm_epsilon) * gain + shift


def rotary_tables(places, rot_dims):
    half_rot = rot_dims // 2
    frequency = jnp.power(10000.0, -2.0 * jnp.arange(half_rot).astype(jnp.float32) / rot_dims)
    phases = places.astype(jnp.float32)[:, None] * frequency[None, :]
    cosine_table = jnp.concatenate([jnp.cos(phases), jnp.cos(phases)], -1)[:, None, :]
    sine_table = jnp.concatenate([jnp.sin(phases), jnp.sin(phases)], -1)[:, None, :]
    return (cosine_table, sine_table)


def rotate(values, cosine_table, sine_table):
    rot_dims = cosine_table.shape[-1]
    half_rot = rot_dims // 2
    rotated_part = values[..., :rot_dims]
    turned = jnp.concatenate([-rotated_part[..., half_rot:], rotated_part[..., :half_rot]], -1)
    return jnp.concatenate(
        [rotated_part * cosine_table + turned * sine_table, values[..., rot_dims:]], -1
    )


def allowed_block(segment_ids, positions, begin_row, block_rows):
    seg_rows = lax.dynamic_slice_in_dim(segment_ids, begin_row, block_rows)
    place_rows = lax.dynamic_slice_in_dim(positions, begin_row, block_rows)
    return (seg_rows[:, None] == segment_ids[None, :]) & (positions[None, :] <= place_rows[:, None])


def block_scores(query_block, keys_low, allowed):
    scores = (
        jnp.einsum("qhe,khe->hqk", query_block, keys_low, preferred_element_type=jnp.float32)
        * 0.125
    )
    return jnp.where(allowed[None], scores, masked_score)


def up_projection(gathered, up_weight, up_bias):
    up_input = jnp.dot(gathered, up_weight, preferred_element_type=jnp.float32) + up_bias.astype(
        jnp.float32
    )
    return (up_input, jax.nn.gelu(up_input, approximate=True).astype(jnp.bfloat16))


def row_product(left, right):
    return jnp.dot(left, right, preferred_element_type=jnp.float32)


def shards(
    tokens,
    upstream,
    segment_ids,
    positions,
    norm_gain,
    norm_bias,
    qkv_weight,
    qkv_bias,
    dense_weight,
    up_weight,
    up_bias,
    down_weight,
    out_bias,
):
    head_count = qkv_weight.shape[2] // HEAD_DIM
    inputs = tokens.astype(jnp.float32)
    normed_low = layer_norm(inputs, norm_gain, norm_bias).astype(jnp.bfloat16)
    gathered = lax.all_gather(normed_low, "tp", axis=0, tiled=True)
    group_rows = gathered.shape[0]
    block_rows = math.gcd(group_rows, 512)
    block_count = group_rows // block_rows
    projected = (
        jnp.einsum("td,dch->tch", gathered, qkv_weight, preferred_element_type=jnp.float32)
        + qkv_bias.astype(jnp.float32)[None]
    )
    head_shape = (group_rows, head_count, HEAD_DIM)
    cosine_table, sine_table = rotary_tables(positions, ROT)
    queries = rotate(projected[:, 0].reshape(head_shape), cosine_table, sine_table).astype(
        jnp.bfloat16
    )
    keys_low = rotate(projected[:, 1].reshape(head_shape), cosine_table, sine_table).astype(
        jnp.bfloat16
    )
    values_low = projected[:, 2].reshape(head_shape).astype(jnp.bfloat16)

    def forward_block(block_index):
        begin_row = block_index * block_rows
        query_block = lax.dynamic_slice_in_dim(queries, begin_row, block_rows, 0)
        scores = block_scores(
            query_block, keys_low, allowed_block(segment_ids, positions, begin_row, block_rows)
        )
        highest_score = jnp.max(scores, -1, keepdims=True)
        exponent = jnp.exp(scores - highest_score)
        totals = jnp.sum(exponent, -1, keepdims=True)
        soft_low = (exponent / totals).astype(jnp.bfloat16)
        context_block = jnp.einsum(
            "hqk,khe->qhe", soft_low, values_low, preferred_element_type=jnp.float32
        )
        return (context_block.astype(jnp.bfloat16), highest_score + jnp.log(totals))

    context_blocks, log_blocks = lax.map(forward_block, jnp.arange(block_count, dtype=jnp.int32))
    context_low = context_blocks.reshape(group_rows, head_count * HEAD_DIM)
    up_input, up_active_low = up_projection(gathered, up_weight, up_bias)
    summed = lax.psum_scatter(
        row_product(context_low, dense_weight) + row_product(up_active_low, down_weight),
        "tp",
        scatter_dimension=0,
        tiled=True,
    )
    mixed = (inputs + summed + out_bias).astype(jnp.bfloat16)
    upstream_all = lax.all_gather(upstream, "tp", axis=0, tiled=True)
    unit_column = jnp.ones((group_rows,), jnp.bfloat16)
    out_bias_grad = jnp.einsum(
        "t,td->d", unit_column, upstream_all, preferred_element_type=jnp.float32
    )
    dense_weight_grad = jnp.einsum(
        "te,td->ed", context_low, upstream_all, preferred_element_type=jnp.float32
    )
    down_weight_grad = jnp.einsum(
        "tf,td->fd", up_active_low, upstream_all, preferred_element_type=jnp.float32
    )
    context_grad = jnp.einsum(
        "td,ed->te", upstream_all, dense_weight, preferred_element_type=jnp.float32
    )
    context_grad_low = context_grad.astype(jnp.bfloat16).reshape(head_shape)
    active_grad = jnp.einsum(
        "td,fd->tf", upstream_all, down_weight, preferred_element_type=jnp.float32
    )
    _, gelu_back = jax.vjp(partial(jax.nn.gelu, approximate=True), up_input)
    up_input_grad = gelu_back(active_grad)[0].astype(jnp.bfloat16)
    up_bias_grad = jnp.einsum(
        "t,tf->f", unit_column, up_input_grad, preferred_element_type=jnp.float32
    )

    def backward_block(running, block_index):
        key_grad, value_grad = running
        begin_row = block_index * block_rows
        query_block = lax.dynamic_slice_in_dim(queries, begin_row, block_rows, 0)
        output_grad = lax.dynamic_slice_in_dim(context_grad_low, begin_row, block_rows, 0)
        log_totals = lax.dynamic_index_in_dim(log_blocks, block_index, 0, keepdims=False)
        scores = block_scores(
            query_block, keys_low, allowed_block(segment_ids, positions, begin_row, block_rows)
        )
        attn_soft = jnp.exp(scores - log_totals)
        value_grad = value_grad + jnp.einsum(
            "hqk,qhe->khe",
            attn_soft.astype(jnp.bfloat16),
            output_grad,
            preferred_element_type=jnp.float32,
        )
        prob_grad = jnp.einsum(
            "qhe,khe->hqk", output_grad, values_low, preferred_element_type=jnp.float32
        )
        row_dots = jnp.sum(attn_soft * prob_grad, -1, keepdims=True)
        score_grad = (attn_soft * (prob_grad - row_dots)).astype(jnp.bfloat16)
        query_grad = (
            jnp.einsum("hqk,khe->qhe", score_grad, keys_low, preferred_element_type=jnp.float32)
            * 0.125
        )
        key_grad = (
            key_grad
            + jnp.einsum(
                "hqk,qhe->khe", score_grad, query_block, preferred_element_type=jnp.float32
            )
            * 0.125
        )
        return ((key_grad, value_grad), query_grad)

    empty_grad = jnp.zeros(head_shape, jnp.float32)
    (key_grad, value_grad), query_blocks = lax.scan(
        backward_block, (empty_grad, empty_grad), jnp.arange(block_count, dtype=jnp.int32)
    )
    query_grad = query_blocks.reshape(head_shape)
    projected_grad = jnp.stack(
        [
            rotate(query_grad, cosine_table, -sine_table),
            rotate(key_grad, cosine_table, -sine_table),
            value_grad,
        ],
        axis=1,
    )
    projected_grad = projected_grad.reshape(group_rows, 3, head_count * HEAD_DIM).astype(
        jnp.bfloat16
    )
    qkv_bias_grad = jnp.einsum(
        "t,tch->ch", unit_column, projected_grad, preferred_element_type=jnp.float32
    )
    qkv_weight_grad = jnp.einsum(
        "td,tch->dch", gathered, projected_grad, preferred_element_type=jnp.float32
    )
    up_weight_grad = jnp.einsum(
        "td,tf->df", gathered, up_input_grad, preferred_element_type=jnp.float32
    )
    first = jnp.einsum(
        "tch,dch->td", projected_grad, qkv_weight, preferred_element_type=jnp.float32
    )
    normed_grad = lax.psum_scatter(
        first
        + jnp.einsum("tf,df->td", up_input_grad, up_weight, preferred_element_type=jnp.float32),
        "tp",
        scatter_dimension=0,
        tiled=True,
    )
    _, norm_back = jax.vjp(layer_norm, inputs, norm_gain, norm_bias)
    input_part, gain_part, shift_part = norm_back(normed_grad)
    input_grad = upstream.astype(jnp.float32) + input_part
    norm_gain_grad, norm_bias_grad = lax.psum((gain_part, shift_part), ("dp", "tp"))
    (
        qkv_weight_grad,
        qkv_bias_grad,
        dense_weight_grad,
        up_weight_grad,
        up_bias_grad,
        down_weight_grad,
        out_bias_grad,
    ) = lax.psum(
        (
            qkv_weight_grad,
            qkv_bias_grad,
            dense_weight_grad,
            up_weight_grad,
            up_bias_grad,
            down_weight_grad,
            out_bias_grad,
        ),
        "dp",
    )
    return (
        mixed,
        input_grad,
        norm_gain_grad,
        norm_bias_grad,
        qkv_weight_grad,
        qkv_bias_grad,
        dense_weight_grad,
        up_weight_grad,
        up_bias_grad,
        down_weight_grad,
        out_bias_grad,
    )


def solution(mesh):
    return jax.shard_map(
        shards,
        mesh=mesh,
        in_specs=(
            P(("dp", "tp"), None),
            P(("dp", "tp"), None),
            P("dp"),
            P("dp"),
            P(),
            P(),
            P(None, None, "tp"),
            P(None, "tp"),
            P("tp", None),
            P(None, "tp"),
            P("tp"),
            P("tp", None),
            P(),
        ),
        out_specs=(
            P(("dp", "tp"), None),
            P(("dp", "tp"), None),
            P(),
            P(),
            P(None, None, "tp"),
            P(None, "tp"),
            P("tp", None),
            P(None, "tp"),
            P("tp"),
            P("tp", None),
            P(),
        ),
        check_vma=False,
    )
```

profile of v0, /device:TPU:0, one launch (start us, length us, event | category | flops | bytes accessed | tf_op | source)
XLA Modules:
  0.0 1277.2 jit_solution(17273535150324957371)
XLA Ops:
  19.3 32.1 %all-gather.3.cloned.1.call-done = bf16[512,2048]{1,0:T(8,128)(2,1)} async-done(((bf16[128,2048]{1,0:T(8,128)(2,1)}), bf16[512,2048]{1,0:T(8,128)(2,1)}) %all-gather.3.cloned.1.call-update) | async-done | bytes 2097168 | tf_op jit(solution)/shard_map/all_gather | solution.py:86
  51.4 6.3 fusion.17
  63.9 24.7 %all-gather.5.cloned.1.call-done = bf16[512,2048]{1,0:T(8,128)(2,1)} async-done(((bf16[128,2048]{1,0:T(8,128)(2,1)}), bf16[512,2048]{1,0:T(8,128)(2,1)}) %all-gather.5.cloned.1.call-update) | async-done | bytes 2097168 | tf_op jit(solution)/shard_map/all_gather | solution.py:129
  88.6 3.0 convolution_convert_fusion
  91.6 5.8 fusion.27
  99.7 2.6 multiply_convert_fusion
  107.1 7.3 fusion.67
  114.4 11.8 fusion.8
  126.2 10.6 fusion.68
  145.2 9.8 bitcast_add_fusion
  156.1 5.1 fusion.26
  161.2 8.4 fusion.63
  169.5 3.4 convolution_add_fusion
  174.7 3.3 fusion.69
  178.0 6.9 fusion.13
  184.9 8.6 fusion.70
  193.5 8.9 fusion.62
  206.5 29.4 %all-reduce.1 = (f32[3,512]{1,0:T(4,128)}, f32[2048]{0:T(1024)}, f32[2048]{0:T(1024)}) all-reduce(f32[3,512]{1,0:T(4,128)S(1)} %bitcast.78, f32[2048]{0:T(1024)S(1)} %bitcast.76, f32[2048]{0:T(1024)S(1)} %bitcast.77), channel_id=1, replica_groups=mesh['dp'=8,'tp'=4] {'dp'}, use_global_device_ids=true, to_apply=%region_14.15 | all-reduce | flops 5632 | bytes 45056 | tf_op jit(solution)/shard_map/psum | solution.py:234
  239.2 37.1 %all-reduce = (f32[2048]{0:T(1024)}, f32[2048]{0:T(1024)}) all-reduce(f32[2048]{0:T(1024)S(1)} %get-tuple-element.57, f32[2048]{0:T(1024)S(1)} %get-tuple-element.59), channel_id=1, replica_groups=mesh['dp'=8,'tp'=4] {'dp','tp'}, use_global_device_ids=true, to_apply=%region_10.11 | all-reduce | flops 4096 | bytes 32768 | tf_op jit(solution)/shard_map/psum | solution.py:225
  276.4 3.2 add_add_fusion.1
  279.6 955.1 %all-reduce.5.cloned.1.call-done = (f32[2048,3,512]{2,0,1:T(8,128)}, f32[512,2048]{1,0:T(8,128)}, f32[2048,2048]{1,0:T(8,128)}, f32[2048,2048]{1,0:T(8,128)}) async-done(((f32[2048,3,512]{2,0,1:T(8,128)}, f32[512,2048]{1,0:T(8,128)}, f32[2048,2048]{1,0:T(8,128)}, f32[2048,2048]{1,0:T(8,128)}), (f32[2048,3,512]{2,0,1:T(8,128)}, f32[512,2048]{1,0:T(8,128)}, f32[2048,2048]{1,0:T(8,128)}, ...) | async-done | bytes 50331664 | tf_op jit(solution)/shard_map/psum | solution.py:234
  1234.7 11.1 copy.47
  1247.9 14.0 %copy.49 = f32[2048,2048]{1,0:T(8,128)} copy(f32[2048,2048]{1,0:T(8,128)} %get-tuple-element.115) | data formatting | bytes 33554432
  1264.0 6.3 copy.50
  (159 shorter events, 48.0 us)
Async XLA Ops:
  7.2 81.4 %copy-start = (bf16[512,2048]{1,0:T(8,128)(2,1)S(1)}, bf16[512,2048]{1,0:T(8,128)(2,1)}, u32[]{:S(2)}) copy-start(bf16[512,2048]{1,0:T(8,128)(2,1)} %param.21) | copy-start | bytes 6291460
  7.2 44.2 %all-gather.3.cloned.1.call-start = ((), (), s32[]{:S(2)}) async-start(), calls=%async_computation.2 | async-start | bytes 2621440 | tf_op jit(solution)/shard_map/all_gather | solution.py:86
  13.2 75.4 %all-gather.5.cloned.1.call-start = ((), (), s32[]{:S(2)}) async-start(), calls=%async_computation.4 | async-start | bytes 2621440 | tf_op jit(solution)/shard_map/all_gather | solution.py:129
  14.0 221.9 %reduce-scatter.5.cloned.1.call-start = ((), (), s32[]{:S(2)}) async-start(), calls=%async_computation.5 | async-start | bytes 5242880 | tf_op jit(solution)/shard_map/reduce_scatter | solution.py:215
  57.8 39.7 %copy-start.10 = (bf16[512,1,512]{0,2,1:T(8,128)(2,1)}, bf16[512,1,512]{0,2,1:T(8,128)(2,1)S(1)}, u32[]{:S(2)}) copy-start(bf16[512,1,512]{0,2,1:T(8,128)(2,1)S(1)} %slice.137) | copy-start | bytes 1572868
  63.9 33.5 %copy-start.29 = (f32[8,512]{1,0:T(8,128)}, f32[8,512]{1,0:T(8,128)S(1)}, u32[]{:S(2)}) copy-start(f32[8,512]{1,0:T(8,128)S(1)} %fusion) | copy-start | bytes 49156
  88.6 8.8 slice-start
  104.5 9.9 copy-start.7
  114.3 11.8 copy-start.42
  126.1 10.7 copy-start.12
  155.1 121.3 %reduce-scatter.3.cloned.1.call-start = ((), (), s32[]{:S(2)}) async-start(), calls=%async_computation.3 | async-start | bytes 5242880 | tf_op jit(solution)/shard_map/reduce_scatter | solution.py:122
  172.9 1061.8 %all-reduce.5.cloned.1.call-start = ((), (), s32[]{:S(2)}) async-start(), calls=%async_computation.6 | async-start | bytes 100663296 | tf_op jit(solution)/shard_map/psum | solution.py:234
  203.6 32.3 %copy-start.3 = (bf16[128,2048]{1,0:T(8,128)(2,1)S(1)}, bf16[128,2048]{1,0:T(8,128)(2,1)}, u32[]{:S(2)}) copy-start(bf16[128,2048]{1,0:T(8,128)(2,1)} %param.13) | copy-start | bytes 1572868
  203.6 32.3 %copy-start.28 = (f32[2048]{0:T(1024)S(1)}, f32[2048]{0:T(1024)}, u32[]{:S(2)}) copy-start(f32[2048]{0:T(1024)} %param.17) | copy-start | bytes 24580
  203.6 32.3 %copy-start.32 = (f32[128]{0:T(128)S(1)}, f32[128]{0:T(128)}, u32[]{:S(2)}) copy-start(f32[128]{0:T(128)} %copy-done.31) | copy-start | bytes 1540
  203.6 33.9 %copy-start.39 = (f32[128]{0:T(128)S(1)}, f32[128]{0:T(128)}, u32[]{:S(2)}) copy-start(f32[128]{0:T(128)} %copy-done.38) | copy-start | bytes 1540
  203.6 33.9 %copy-start.37 = (f32[128]{0:T(128)S(1)}, f32[128]{0:T(128)}, u32[]{:S(2)}) copy-start(f32[128]{0:T(128)} %copy-done.36) | copy-start | bytes 1540
  203.9 72.5 %copy-start.9 = (bf16[128,2048]{1,0:T(8,128)(2,1)S(1)}, bf16[128,2048]{1,0:T(8,128)(2,1)}, u32[]{:S(2)}) copy-start(bf16[128,2048]{1,0:T(8,128)(2,1)} %param.14) | copy-start | bytes 1572868
  203.9 72.5 %copy-start.33 = (f32[2048]{0:T(1024)S(1)}, f32[2048]{0:T(1024)}, u32[]{:S(2)}) copy-start(f32[2048]{0:T(1024)} %param.25) | copy-start | bytes 24580
  1234.7 11.1 copy-start.8
  1245.8 16.2 %slice-start.2 = ((s8[16777216]{0:T(1024)(128)(4,1)}), s8[4194304]{0:T(1024)(128)(4,1)S(1)}, s32[]{:S(2)}) async-start(s8[16777216]{0:T(1024)(128)(4,1)} %bitcast.59), calls=%async_computation.9 | async-start | bytes 8388608
  1247.9 14.0 %slice-start.3 = ((s8[16777216]{0:T(1024)(128)(4,1)}), s8[4194304]{0:T(1024)(128)(4,1)S(1)}, s32[]{:S(2)}) async-start(s8[16777216]{0:T(1024)(128)(4,1)} %bitcast.59), calls=%async_computation.10 | async-start | bytes 8388608
  1247.9 14.0 %slice-start.4 = ((s8[16777216]{0:T(1024)(128)(4,1)}), s8[4194304]{0:T(1024)(128)(4,1)S(1)}, s32[]{:S(2)}) async-start(s8[16777216]{0:T(1024)(128)(4,1)} %bitcast.59), calls=%async_computation.11 | async-start | bytes 8388608
  1247.9 16.0 %slice-start.5 = ((s8[16777216]{0:T(1024)(128)(4,1)}), s8[4194304]{0:T(1024)(128)(4,1)S(1)}, s32[]{:S(2)}) async-start(s8[16777216]{0:T(1024)(128)(4,1)} %bitcast.59), calls=%async_computation.12 | async-start | bytes 8388608
  (32 other events, 105.0 us)
Sparse Core Ops, SparseCore 0:
  13.4 38.0 all-gather.2
  53.3 35.2 all-gather.4
  155.2 52.6 reduce-scatter.4
  211.0 53.1 reduce-scatter.2
  268.1 966.5 all-reduce.4
where the time goes:
time: 1290 us; the launch traced here: 1280 us
  waiting for transfers between devices  1010 us (78%)
  matrix products  108 us (8%)
  blocking collectives  66.5 us (5%)
  local copies, waits for them, and re-layouts  48.4 us (4%)
  other arithmetic  27 us (2%)
  between operations  14.8 us (1%)
    psum x1, waiting for transfers between devices, shards(): lax.psum((qkv_weight_grad, qkv_bias_grad, dense_weight_grad, up_weight_gr...  955 us
    unnamed x106, local copies, waits for them, and re-layouts  43.2 us
    psum x1, blocking collectives, shards(): lax.psum((gain_part, shift_part), ('dp', 'tp'))  37.1 us
    all_gather x1, waiting for transfers between devices, shards(): gathered = lax.all_gather(normed_low, 'tp', axis=0, tiled=True)  32.1 us
    psum x1, blocking collectives, shards(): lax.psum((qkv_weight_grad, qkv_bias_grad, dense_weight_grad, up_weight_gr...  29.4 us
  transfers between devices with their start and end apart: 5, of which 3 were waited for; matrix products, arithmetic and copies ran while one was open for 5% of the time, Pallas kernels for 0%

commit v1 on v0

--- a/solution.py
+++ b/solution.py
@@ -4,14 +4,24 @@
 import jax
 import jax.numpy as jnp
 from jax import lax
+from jax.experimental import pallas as pl
+from jax.experimental.pallas import tpu as pltpu
 from jax.sharding import PartitionSpec as P
 
 HEAD_DIM = 64
 ROT = 32
-
-
 norm_epsilon = 1e-05
 masked_score = -1e30
+low = jnp.bfloat16
+wide = jnp.float32
+VMEM = 56 * 2**20
+HASTE = 0.1
+
+
+def dot(left, right, left_dim, right_dim, kind=wide):
+    return lax.dot_general(
+        left, right, (((left_dim,), (right_dim,)), ((), ())), preferred_element_type=wide
+    ).astype(kind)
 
 
 def layer_norm(values, gain, shift):
@@ -23,8 +33,8 @@
 
 def rotary_tables(places, rot_dims):
     half_rot = rot_dims // 2
-    frequency = jnp.power(10000.0, -2.0 * jnp.arange(half_rot).astype(jnp.float32) / rot_dims)
-    phases = places.astype(jnp.float32)[:, None] * frequency[None, :]
+    frequency = jnp.power(10000.0, -2.0 * jnp.arange(half_rot).astype(wide) / rot_dims)
+    phases = places.astype(wide)[:, None] * frequency[None, :]
     cosine_table = jnp.concatenate([jnp.cos(phases), jnp.cos(phases)], -1)[:, None, :]
     sine_table = jnp.concatenate([jnp.sin(phases), jnp.sin(phases)], -1)[:, None, :]
     return (cosine_table, sine_table)
@@ -40,6 +50,526 @@
     )
 
 
+def gelu_and_slope(v):
+    inner = jnp.tanh(0.7978845608 * (v + 0.044715 * v * v * v))
+    half = 0.5 * (1.0 + inner)
+    slope = half + 0.5 * v * (1.0 - inner * inner) * 0.7978845608 * (1.0 + 0.134145 * v * v)
+    return v * half, slope
+
+
+def kernel_call(body, flops, out_shape, **kinds):
+    return pl.pallas_call(
+        body,
+        out_shape=out_shape,
+        compiler_params=pltpu.CompilerParams(vmem_limit_bytes=VMEM),
+        cost_estimate=pl.CostEstimate(
+            flops=int(flops * HASTE), bytes_accessed=int(flops * HASTE) // 512, transcendentals=0
+        ),
+        **kinds,
+    )
+
+
+def sds(shape, kind):
+    return jax.ShapeDtypeStruct(shape, kind)
+
+
+def whole_block(array):
+    zeros = (0,) * array.ndim
+    return pl.BlockSpec(array.shape, lambda *_: zeros, pipeline_mode=pl.Buffered(1))
+
+
+def fixed_block(shape):
+    zeros = (0,) * len(shape)
+    return pl.BlockSpec(shape, lambda *_: zeros)
+
+
+def assemble(target, pieces):
+    at = 0
+    for ref, first, size in pieces:
+        target[at : at + size, :] = ref[first : first + size, :]
+        at += size
+
+
+def turned(values, cosine, sine_low, sine_high):
+    return (
+        values * cosine
+        + pltpu.roll(values, 128 - ROT // 2, 1) * sine_low
+        + pltpu.roll(values, ROT // 2, 1) * sine_high
+    )
+
+
+def row_means(inputs):
+    centred = inputs - jnp.mean(inputs, -1, keepdims=True)
+    spread = jnp.mean(centred * centred, -1, keepdims=True)
+    scale = lax.rsqrt(spread + norm_epsilon)
+    return centred * scale, scale
+
+
+def norm_kernel(tokens, upstream, gain, shift, normed, both):
+    unit, _ = row_means(tokens[...].astype(wide))
+    rows = tokens.shape[0]
+    normed[...] = (unit * gain[...] + shift[...]).astype(low)
+    both[:rows, :] = normed[...]
+    both[rows:, :] = upstream[...]
+
+
+def norm_rows(tokens, upstream, gain, shift):
+    rows, features = tokens.shape
+    arrays = [tokens, upstream, gain, shift]
+    return kernel_call(
+        norm_kernel,
+        rows * features * 512,
+        [sds((rows, features), low), sds((2 * rows, features), low)],
+        grid=(1,),
+        in_specs=[whole_block(a) for a in arrays],
+        out_specs=[fixed_block((rows, features)), fixed_block((2 * rows, features))],
+    )(*arrays)
+
+
+def norm_back_kernel(tokens, upstream, gain, out_bias, own, got_1, got_2, got_3, mixed, input_grad, sums):
+    rows = tokens.shape[0]
+    inputs, cotangent = tokens[...].astype(wide), upstream[...].astype(wide)
+
+    def total(first):
+        span = slice(first, first + rows)
+        return (own[span, :] + got_1[span, :].astype(wide)) + (
+            got_2[span, :].astype(wide) + got_3[span, :].astype(wide)
+        )
+
+    mixed[...] = (inputs + total(0) + out_bias[...]).astype(low)
+    unit, scale = row_means(inputs)
+    normed_grad = total(rows)
+    e = normed_grad * gain[...]
+    along = jnp.mean(e * unit, -1, keepdims=True)
+    input_grad[...] = cotangent + (e - jnp.mean(e, -1, keepdims=True) - unit * along) * scale
+    sums[0:1, :] = jnp.sum(normed_grad * unit, 0, keepdims=True)
+    sums[1:2, :] = jnp.sum(normed_grad, 0, keepdims=True)
+    sums[2:3, :] = jnp.sum(cotangent, 0, keepdims=True)
+
+
+def norm_back(*arrays):
+    rows, features = arrays[0].shape
+    shapes = [(rows, features), (rows, features), (3, features)]
+    return kernel_call(
+        norm_back_kernel,
+        rows * features * 1024,
+        [sds(s, k) for s, k in zip(shapes, (low, wide, wide))],
+        grid=(1,),
+        in_specs=[whole_block(a) for a in arrays],
+        out_specs=[fixed_block(s) for s in shapes],
+    )(*arrays)
+
+
+def project_kernel(count, *refs):
+    weight, bias, cosine, sine_low, sine_high, rows_out, out = refs[count:]
+    part = pl.program_id(0)
+
+    @pl.when(part == 0)
+    def _():
+        assemble(rows_out, [(r, 0, r.shape[0]) for r in refs[:count]])
+
+    projected = dot(rows_out[...], weight[0], 1, 0) + bias[0].astype(wide)
+
+    @pl.when(part < 2)
+    def _():
+        scale = jnp.where(part == 0, 0.125, 1.0)
+        for j in range(0, projected.shape[1], 128):
+            rotated = turned(projected[:, j : j + 128], cosine[...], sine_low[...], sine_high[...])
+            out[0, :, j : j + 128] = (rotated * scale).astype(low)
+
+    @pl.when(part == 2)
+    def _():
+        out[0] = projected.astype(low)
+
+
+def project(blocks, weight, bias, tables):
+    tokens = sum(b.shape[0] for b in blocks)
+    _, features, width = weight.shape
+    table = whole_block(tables[0])
+    return kernel_call(
+        partial(project_kernel, len(blocks)),
+        6 * tokens * features * width,
+        [sds((tokens, features), low), sds((3, tokens, width), low)],
+        grid=(3,),
+        in_specs=[whole_block(a) for a in blocks]
+        + [
+            pl.BlockSpec((1, features, width), lambda c: (c, 0, 0)),
+            pl.BlockSpec((1, 1, width), lambda c: (c, 0, 0)),
+            table,
+            table,
+            table,
+        ],
+        out_specs=[fixed_block((tokens, features)), pl.BlockSpec((1, tokens, width), lambda c: (c, 0, 0))],
+    )(*blocks, weight, bias, *tables)
+
+
+def attention_kernel(count, *refs):
+    (queries, keys, values, dense, seg_q, place_q, seg_k, place_k, cosine, sine_low, sine_high) = refs[count:-5]
+    rows_out, context, out, bias_out, mask = refs[-5:]
+
+    @pl.when(pl.program_id(0) == 0)
+    def _():
+        assemble(rows_out, [(r, 0, r.shape[0]) for r in refs[:count]])
+        allowed = (seg_q[...] == seg_k[...]) & (place_k[...] <= place_q[...])
+        mask[...] = jnp.where(allowed, 0.0, masked_score)
+
+    q, k, v = queries[0], keys[0], values[0]
+    g = dot(rows_out[...], dense[...], 1, 1, low)
+    lane = lax.broadcasted_iota(jnp.int32, q.shape, 1) // HEAD_DIM
+    found = []
+    for head in range(128 // HEAD_DIM):
+        mine = lane == head
+        scores = dot(jnp.where(mine, q, jnp.zeros_like(q)), k, 1, 1) + mask[...]
+        exponent = jnp.exp(scores - jnp.max(scores, -1, keepdims=True))
+        soft = exponent * (1.0 / jnp.sum(exponent, -1, keepdims=True))
+        soft_low = soft.astype(low)
+        prob_grad = dot(jnp.where(mine, g, jnp.zeros_like(g)), v, 1, 1)
+        row_dots = jnp.sum(soft * prob_grad, -1, keepdims=True)
+        score_grad = (soft * (prob_grad - row_dots)).astype(low)
+        found.append(
+            (dot(soft_low, v, 1, 0), dot(score_grad, k, 1, 0), dot(score_grad, q, 0, 0), dot(soft_low, g, 0, 0))
+        )
+    parts = [jnp.where(lane == 0, a, b) for a, b in zip(*found)]
+    context[...] = parts[0].astype(low)
+    back = (cosine[...], -sine_low[...], -sine_high[...])
+    grads = [turned(parts[1] * 0.125, *back), turned(parts[2], *back), parts[3]]
+    for c, value in enumerate(grads):
+        rounded = value.astype(low)
+        out[c] = rounded
+        bias_out[c] = jnp.sum(rounded.astype(wide), 0, keepdims=True)
+
+
+def attention(blocks, qkv, dense_weight, seg, place, tables):
+    _, tokens, width = qkv.shape
+    features = dense_weight.shape[1]
+    column, row = (lambda a: a.reshape(tokens, 1)), (lambda a: a.reshape(1, tokens))
+    extras = [column(seg), column(place), row(seg), row(place), *tables]
+    part = lambda c: pl.BlockSpec((1, tokens, 128), lambda j: (c, 0, j))
+    return kernel_call(
+        partial(attention_kernel, len(blocks)),
+        20 * tokens * tokens * width,
+        [
+            sds((tokens, features), low),
+            sds((tokens, width), low),
+            sds((3, tokens, width), low),
+            sds((3, 1, width), wide),
+        ],
+        grid=(width // 128,),
+        in_specs=[whole_block(b) for b in blocks]
+        + [part(0), part(1), part(2), pl.BlockSpec((128, features), lambda j: (j, 0))]
+        + [whole_block(e) for e in extras],
+        out_specs=[
+            fixed_block((tokens, features)),
+            pl.BlockSpec((tokens, 128), lambda j: (0, j)),
+            pl.BlockSpec((3, tokens, 128), lambda j: (0, 0, j)),
+            pl.BlockSpec((3, 1, 128), lambda j: (0, 0, j)),
+        ],
+        scratch_shapes=[pltpu.VMEM((tokens, tokens), wide)],
+    )(*blocks, qkv, qkv, qkv, dense_weight, *extras)
+
+
+def outer_parts_kernel(left, right, out):
+    out[0] = dot(left[...], right[0], 0, 0, low)
+
+
+def outer_parts(left, right, tile=1024):
+    count, tokens, n = right.shape
+    m = left.shape[1]
+    return kernel_call(
+        outer_parts_kernel,
+        2 * count * tokens * m * n,
+        sds((count, m, n), low),
+        grid=(m // tile, count),
+        in_specs=[
+            pl.BlockSpec((tokens, tile), lambda i, c: (0, i)),
+            pl.BlockSpec((1, tokens, n), lambda i, c: (c, 0, 0)),
+        ],
+        out_specs=pl.BlockSpec((1, tile, n), lambda i, c: (c, i, 0)),
+    )(left, right)
+
+
+def feed_kernel(layouts, n_arrays, *refs):
+    arrays, refs = refs[:n_arrays], refs[n_arrays:]
+    up_weight, down_weight, up_bias = refs[:3]
+    outs = refs[3:]
+    pick = lambda layout: [(arrays[i], first, size) for i, first, size in layout]
+
+    @pl.when(pl.program_id(0) == 0)
+    def _():
+        for (normed_layout, upstream_layout), (normed_out, upstream_out, *_) in zip(layouts, fives(outs)):
+            assemble(normed_out, pick(normed_layout))
+            assemble(upstream_out, pick(upstream_layout))
+
+    bias = up_bias[...].astype(wide)
+    for normed_out, upstream_out, active_out, grad_out, sum_out in fives(outs):
+        active, slope = gelu_and_slope(dot(normed_out[...], up_weight[...], 1, 0) + bias)
+        active_out[...] = active.astype(low)
+        rounded = (dot(upstream_out[...], down_weight[...], 1, 1) * slope).astype(low)
+        grad_out[...] = rounded
+        sum_out[...] = jnp.sum(rounded.astype(wide), 0, keepdims=True)
+
+
+def fives(outs):
+    return [outs[i : i + 5] for i in range(0, len(outs), 5)]
+
+
+def feed(arrays, layouts, up_weight, down_weight, up_bias, tile=512):
+    features, hidden = up_weight.shape
+    tokens = sum(size for _, _, size in layouts[0][0])
+    rows_spec = fixed_block((tokens, features))
+    tile_spec = pl.BlockSpec((tokens, tile), lambda j: (0, j))
+    sum_spec = pl.BlockSpec((1, tile), lambda j: (0, j))
+    shapes = [sds((tokens, features), low)] * 2 + [sds((tokens, hidden), low)] * 2 + [sds((1, hidden), wide)]
+    found = kernel_call(
+        partial(feed_kernel, layouts, len(arrays)),
+        4 * len(layouts) * tokens * features * hidden,
+        shapes * len(layouts),
+        grid=(hidden // tile,),
+        in_specs=[whole_block(a) for a in arrays]
+        + [
+            pl.BlockSpec((features, tile), lambda j: (0, j)),
+            pl.BlockSpec((tile, features), lambda j: (j, 0)),
+            pl.BlockSpec((1, tile), lambda j: (0, j)),
+        ],
+        out_specs=[rows_spec, rows_spec, tile_spec, tile_spec, sum_spec] * len(layouts),
+    )(*arrays, up_weight, down_weight, up_bias)
+    return fives(found)
+
+
+def back_kernel(n_tp, active, context, up_grad, part_grad, down, dense, up, part_weight, own, *sent):
+    rows = active.shape[0] // n_tp
+    mixed = dot(active[...], down[...], 1, 0) + dot(context[...], dense[...], 1, 0)
+    normed_grad = dot(up_grad[...], up[...], 1, 1)
+    for c in range(3):
+        normed_grad = normed_grad + dot(part_grad[c], part_weight[c], 1, 1)
+    for i, value in enumerate((mixed, normed_grad)):
+        span = slice(i * rows, (i + 1) * rows)
+        own[span, :] = value[:rows]
+        for r in range(1, n_tp):
+            sent[r - 1][span, :] = value[r * rows : (r + 1) * rows].astype(low)
+
+
+def back_to_tokens(n_tp, active, context, up_grad, part_grad, down, dense, up, part_weight, tile=512):
+    tokens, hidden = active.shape
+    features, width = down.shape[1], context.shape[1]
+    rows = 2 * tokens // n_tp
+    column = pl.BlockSpec((rows, tile), lambda j: (0, j))
+    return kernel_call(
+        partial(back_kernel, n_tp),
+        4 * tokens * features * (hidden + 2 * width),
+        [sds((rows, features), wide)] + [sds((rows, features), low)] * (n_tp - 1),
+        grid=(features // tile,),
+        in_specs=[whole_block(a) for a in (active, context, up_grad, part_grad)]
+        + [
+            pl.BlockSpec((hidden, tile), lambda j: (0, j)),
+            pl.BlockSpec((width, tile), lambda j: (0, j)),
+            pl.BlockSpec((tile, hidden), lambda j: (j, 0)),
+            pl.BlockSpec((3, tile, width), lambda j: (0, j, 0)),
+        ],
+        out_specs=[column] * n_tp,
+    )(active, context, up_grad, part_grad, down, dense, up, part_weight)
+
+
+def outer_kernel(count, place, *refs):
+    out = refs[2 * count]
+    for here in range(count):
+
+        @pl.when(place[0] == here)
+        def _():
+            total = None
+            for there in range(count):
+                i = here ^ there
+                term = dot(refs[i][...], refs[count + i][...], 0, 0)
+                total = term if total is None else total + term
+            out[...] = total.astype(out.dtype)
+
+
+def outer_sum(place, lefts, rights, tile_m=512, tile_n=1024):
+    count, (tokens, m), n = len(lefts), lefts[0].shape, rights[0].shape[1]
+    return kernel_call(
+        partial(outer_kernel, count),
+        2 * count * tokens * m * n,
+        sds((m, n), low),
+        grid_spec=pltpu.PrefetchScalarGridSpec(
+            num_scalar_prefetch=1,
+            grid=(n // tile_n, m // tile_m),
+            in_specs=[pl.BlockSpec((tokens, tile_m), lambda j, i, _: (0, i))] * count
+            + [pl.BlockSpec((tokens, tile_n), lambda j, i, _: (0, j))] * count,
+            out_specs=pl.BlockSpec((tile_m, tile_n), lambda j, i, _: (i, j)),
+        ),
+    )(place.reshape(1).astype(jnp.int32), *lefts, *rights)
+
+
+def add_kernel(*refs):
+    total = refs[0][...].astype(wide)
+    for ref in refs[1:-1]:
+        total = total + ref[...].astype(wide)
+    refs[-1][...] = total
+
+
+def added(*terms, tile=512):
+    m, n = terms[0].shape
+    spec = pl.BlockSpec((tile, n), lambda i: (i, 0))
+    return kernel_call(
+        add_kernel, m * n * 256, sds((m, n), wide), grid=(m // tile,), in_specs=[spec] * len(terms), out_specs=spec
+    )(*terms)
+
+
+def tie(*arrays):
+    return lax.optimization_barrier(arrays)
+
+
+def shards(
+    tokens,
+    upstream,
+    segment_ids,
+    positions,
+    norm_gain,
+    norm_bias,
+    qkv_weight,
+    qkv_bias,
+    dense_weight,
+    up_weight,
+    up_bias,
+    down_weight,
+    out_bias,
+):
+    n_tp, n_line = 4, 4
+    dp_place, tp_place = lax.axis_index("dp"), lax.axis_index("tp")
+    line_place = dp_place // 2
+    rows, features = tokens.shape
+    group_rows = rows * n_tp
+    heads_wide = qkv_weight.shape[2]
+    hidden = up_weight.shape[1]
+
+    def swap_tp(array, flip):
+        return lax.ppermute(array, "tp", [(i, i ^ flip) for i in range(n_tp)])
+
+    def swap_core(array):
+        return lax.ppermute(array, "dp", [(i, i ^ 1) for i in range(2 * n_line)])
+
+    def swap_line(array, flip):
+        return lax.ppermute(array, "dp", [(i, i ^ (2 * flip)) for i in range(2 * n_line)])
+
+    def hop(array, pairs):
+        return lax.ppermute(array, "dp", [(2 * s + c, 2 * d + c) for s, d in pairs for c in (0, 1)])
+
+    def from_others(array):
+        return [swap_tp(array, r) for r in range(1, n_tp)]
+
+    gain, shift, last_bias = (a.reshape(1, features) for a in (norm_gain, norm_bias, out_bias))
+    normed, both = norm_rows(tokens, upstream, gain, shift)
+    normed_blocks = [normed, *from_others(normed)]
+    above_1, below_1 = hop(both, [(0, 1), (1, 2), (2, 3)]), hop(both, [(1, 0), (2, 1), (3, 2)])
+
+    by_owner = jnp.stack([segment_ids.reshape(n_tp, rows), positions.reshape(n_tp, rows)])
+    owner = tp_place ^ jnp.arange(n_tp)
+    pick = (owner[:, None] == jnp.arange(n_tp)[None, :]).astype(jnp.int32)
+    arranged = jnp.sum(pick[None, :, :, None] * by_owner[:, None, :, :], 2).reshape(2, group_rows)
+    seg, place = arranged[0], arranged[1]
+    cosine_table, sine_table = rotary_tables(place, ROT)
+    cosine, sine = cosine_table[:, 0, :], sine_table[:, 0, :]
+    still = jnp.zeros((group_rows, HEAD_DIM - ROT), wide)
+    quiet = jnp.zeros((group_rows, ROT // 2), wide)
+    tables = [
+        jnp.concatenate([cosine, still + 1.0], 1),
+        jnp.concatenate([-sine[:, : ROT // 2], quiet, still], 1),
+        jnp.concatenate([quiet, sine[:, : ROT // 2], still], 1),
+    ]
+    tables = [jnp.concatenate([t] * (128 // HEAD_DIM), 1) for t in tables]
+    parts_weight = qkv_weight.transpose(1, 0, 2)
+    parts_bias = qkv_bias.reshape(3, 1, heads_wide)
+
+    normed_blocks, tables, late_upstream, seg, place, above_1, below_1 = tie(
+        normed_blocks, tables, upstream, seg, place, above_1, below_1
+    )
+    above_2, below_2 = hop(above_1, [(1, 2), (2, 3)]), hop(below_1, [(1, 0), (2, 1)])
+    slot_1 = jnp.where(line_place % 2 == 1, above_1, below_1)
+    upstream_blocks = [late_upstream, *from_others(late_upstream)]
+    group_normed, qkv = project(normed_blocks, parts_weight, parts_bias, tables)
+
+    upstream_blocks, slot_1, above_2, below_2, group_normed, qkv = tie(
+        upstream_blocks, slot_1, above_2, below_2, group_normed, qkv
+    )
+    above_3, below_3 = hop(above_2, [(2, 3)]), hop(below_2, [(1, 0)])
+    slot_2 = jnp.where(line_place >= 2, above_2, below_2)
+    slot_1 = [slot_1, *from_others(slot_1)]
+    group_upstream, context, projected_grad, qkv_bias_grad = attention(
+        upstream_blocks, qkv, dense_weight, seg, place, tables
+    )
+    qkv_part = outer_parts(group_normed, projected_grad)
+    dense_part = outer_sum(0 * line_place, [context], [group_upstream], heads_wide, features // 2)
+    qkv_sum, dense_sum = lax.psum((qkv_part, dense_part), "dp")
+
+    slot_layout = (
+        [(i, 0, rows) for i in range(n_tp)],
+        [(i, rows, rows) for i in range(n_tp)],
+    )
+    weights = (up_weight, down_weight, up_bias.reshape(1, hidden))
+    slot_3 = jnp.where(
+        line_place == 0, below_3, jnp.where(line_place == 1, below_1, jnp.where(line_place == 2, above_1, above_3))
+    )
+    slot_1, slot_2, slot_3, group_upstream, context, projected_grad, _, _ = tie(
+        slot_1, slot_2, slot_3, group_upstream, context, projected_grad, qkv_part, dense_part
+    )
+    slot_2 = [slot_2, *from_others(slot_2)]
+    own_layout = ([(n_tp, 0, group_rows)], [(n_tp + 1, 0, group_rows)])
+    group_1, group_0 = feed([*slot_1, group_normed, group_upstream], [slot_layout, own_layout], *weights)
+    slot_2, slot_3, group_0, group_1 = tie(slot_2, slot_3, group_0, group_1)
+    slot_3 = [slot_3, *from_others(slot_3)]
+    active, up_input_grad, up_bias_grad = group_0[2:]
+    own_part, *parts = back_to_tokens(
+        n_tp, active, context, up_input_grad, projected_grad, down_weight, dense_weight, up_weight, parts_weight
+    )
+
+    (group_2,) = feed(slot_2, [slot_layout], *weights)
+
+    slot_3, parts, group_2 = tie(slot_3, parts, group_2)
+    got = [swap_tp(part, r + 1) for r, part in enumerate(parts)]
+    (group_3,) = feed(slot_3, [slot_layout], *weights)
+
+    groups = [group_0, group_1, group_2, group_3]
+    normeds, upstreams, actives, up_grads = ([g[i] for g in groups] for i in range(4))
+    up_part = outer_sum(line_place, normeds, up_grads)
+    got, up_part, own_part, qkv_sum, dense_sum = tie(got, up_part, own_part, qkv_sum, dense_sum)
+    other_up_part = swap_core(up_part)
+
+    mixed, input_grad, sums = norm_back(tokens, upstream, gain, last_bias, own_part, *got)
+    sums = sums + swap_tp(sums, 1)
+    sums = sums + swap_tp(sums, 2)
+    small = jnp.concatenate([sums.reshape(1, -1), qkv_bias_grad.reshape(1, -1), up_bias_grad], 1)
+    small = small + swap_core(small)
+    small = small + swap_line(small, 1)
+    small = (small + swap_line(small, 2))[0]
+    norm_gain_grad = small[:features]
+    norm_bias_grad = small[features : 2 * features]
+    out_bias_grad = small[2 * features : 3 * features]
+    qkv_bias_grad = small[3 * features : 3 * features + 3 * heads_wide].reshape(3, heads_wide)
+    up_bias_grad = small[3 * features + 3 * heads_wide :]
+
+    down_part = outer_sum(line_place, actives, upstreams)
+    other_down_part = swap_core(down_part)
+    up_weight_grad = added(up_part, other_up_part)
+    qkv_weight_grad = added(qkv_sum.reshape(3 * features, heads_wide), tile=features)
+    qkv_weight_grad = qkv_weight_grad.reshape(3, features, heads_wide).transpose(1, 0, 2)
+    dense_weight_grad = added(dense_sum)
+    down_weight_grad = added(down_part, other_down_part)
+
+    return (
+        mixed,
+        input_grad,
+        norm_gain_grad,
+        norm_bias_grad,
+        qkv_weight_grad,
+        qkv_bias_grad,
+        dense_weight_grad,
+        up_weight_grad,
+        up_bias_grad,
+        down_weight_grad,
+        out_bias_grad,
+    )
+
+
 def allowed_block(segment_ids, positions, begin_row, block_rows):
     seg_rows = lax.dynamic_slice_in_dim(segment_ids, begin_row, block_rows)
     place_rows = lax.dynamic_slice_in_dim(positions, begin_row, block_rows)
@@ -65,7 +595,7 @@
     return jnp.dot(left, right, preferred_element_type=jnp.float32)
 
 
-def shards(
+def general_shards(
     tokens,
     upstream,
     segment_ids,
@@ -259,8 +789,9 @@
 
 
 def solution(mesh):
+    fits = mesh.shape["dp"] == 8 and mesh.shape["tp"] == 4
     return jax.shard_map(
-        shards,
+        shards if fits else general_shards,
         mesh=mesh,
         in_specs=(
             P(("dp", "tp"), None),

time: 1290 us -> 376 us (0.29)
  waiting for transfers between devices: 1010 us -> 91.8 us
  Pallas kernels: 0 us -> 209 us
  matrix products: 108 us -> 0 us
  blocking collectives: 66.5 us -> 0 us
  starting transfers between devices: 0.2 us -> 41.8 us
  local copies, waits for them, and re-layouts: 48.4 us -> 7.68 us
  other arithmetic: 27 us -> 6.36 us
    psum x1, waiting for transfers between devices: 955 us -> 17 us  [shards(): qkv_sum, dense_sum = lax.psum((qkv_part, dense_part), 'dp')]
    pallas_call x0 -> x16, Pallas kernels: none -> 209 us  [the longest x3 58 us: feed(): kernel_call(partial(feed_kernel, layouts, len(arrays)), 4 * len(layouts)...]
    dot_general x21 -> x0, matrix products: 108 us -> none  [the longest x1 11.8 us: shards(): jnp.einsum('td,fd->tf', upstream_all, down_weight, preferred_element_type...]
    ppermute x0 -> x31, waiting for transfers between devices: none -> 74.7 us  [the longest x20 64.1 us: swap_tp(): return lax.ppermute(array, 'tp', [(i, i ^ flip) for i in range(n_tp)])]
    psum x2 -> x0, blocking collectives: 66.5 us -> none  [the longest x1 37.1 us: shards(): lax.psum((gain_part, shift_part), ('dp', 'tp'))]
    all_gather x2 -> x0, waiting for transfers between devices: 56.8 us -> none  [the longest x1 32.1 us: shards(): gathered = lax.all_gather(normed_low, 'tp', axis=0, tiled=True)]
    unnamed x106 -> x47, local copies, waits for them, and re-layouts: 43.2 us -> 0.13 us
    ppermute x0 -> x31, starting transfers between devices: none -> 41.8 us  [the longest x20 25 us: swap_tp(): return lax.ppermute(array, 'tp', [(i, i ^ flip) for i in range(n_tp)])]
  transfers between devices with their start and end apart: 5 -> 32, of which waited for: 3 -> 19; matrix products, arithmetic and copies ran while one was open for 5% -> 4% of each run, Pallas kernels for 0% -> 52%
where the time goes in v1:
time: 376 us; the launch traced here: 371 us
  Pallas kernels  209 us (56%)
  waiting for transfers between devices  91.8 us (24%)
  starting transfers between devices  41.8 us (11%)
  between operations  14.9 us (4%)
  local copies, waits for them, and re-layouts  7.68 us (2%)
  other arithmetic  6.36 us (2%)
    ppermute x20, waiting for transfers between devices, swap_tp(): return lax.ppermute(array, 'tp', [(i, i ^ flip) for i in range(n_tp)])  64.1 us
    pallas_call x3, Pallas kernels, feed(): kernel_call(partial(feed_kernel, layouts, len(arrays)), 4 * len(layouts)...  58 us
    pallas_call x3, Pallas kernels, outer_sum(): kernel_call(partial(outer_kernel, count), 2 * count * tokens * m * n, sds...  52.4 us
    pallas_call x4, Pallas kernels, added(): kernel_call(add_kernel, m * n * 256, sds((m, n), wide), grid=(m // tile,)...  34.7 us
    ppermute x20, starting transfers between devices, swap_tp(): return lax.ppermute(array, 'tp', [(i, i ^ flip) for i in range(n_tp)])  25 us
    pallas_call x1, Pallas kernels, back_to_tokens(): kernel_call(partial(back_kernel, n_tp), 4 * tokens * features * (hidden +...  19.8 us
    pallas_call x1, Pallas kernels, attention(): kernel_call(partial(attention_kernel, len(blocks)), 20 * tokens * tokens...  17.7 us
    psum x1, waiting for transfers between devices, shards(): qkv_sum, dense_sum = lax.psum((qkv_part, dense_part), 'dp')  17 us
  transfers between devices with their start and end apart: 32, of which 19 were waited for; matrix products, arithmetic and copies ran while one was open for 4% of the time, Pallas kernels for 52%

profile of v1, /device:TPU:0, one launch (start us, length us, event | category | flops | bytes accessed | tf_op | source)
XLA Modules:
  0.0 371.1 jit_solution(10194075584657462130)
XLA Ops:
  10.0 3.9 %collective-permute-start.2 = (bf16[128,2048]{1,0:T(8,128)(2,1)}, bf16[128,2048]{1,0:T(8,128)(2,1)S(1)}, u32[]{:S(2)}, u32[]{:S(2)}) collective-permute-start(bf16[128,2048]{1,0:T(8,128)(2,1)} %get-tuple-element.110.refs_0_), channel_id=1, source_target_pairs={{0,3},{1,2},{2,1},{3,0},{4,7},{5,6},{6,5},{7,4},{8,11},{9,10},{10,... | collective-permute-start | bytes 1572872 | tf_op jit(solution)/shard_map/ppermute | solution.py:446
  15.8 5.6 %collective-permute-start.3 = (bf16[256,2048]{1,0:T(8,128)(2,1)}, bf16[256,2048]{1,0:T(8,128)(2,1)}, u32[]{:S(2)}, u32[]{:S(2)}) collective-permute-start(bf16[256,2048]{1,0:T(8,128)(2,1)} %get-tuple-element.106), channel_id=1, source_target_pairs={{0,8},{4,12},{8,16},{12,20},{16,24},{20,28},{1,9},{5,13},{9,17},{1... | collective-permute-start | bytes 3145736 | tf_op jit(solution)/shard_map/ppermute | solution.py:455
  26.9 10.5 %collective-permute-done.1.refs_2_ = bf16[128,2048]{1,0:T(8,128)(2,1)} collective-permute-done((bf16[128,2048]{1,0:T(8,128)(2,1)}, bf16[128,2048]{1,0:T(8,128)(2,1)}, u32[]{:S(2)}, u32[]{:S(2)}) %collective-permute-start.1) | collective-permute-done | bytes 524320 | tf_op jit(solution)/shard_map/ppermute | solution.py:446
  37.7 3.3 collective-permute-done.4
  49.3 9.1 %shard_map.213 = (bf16[512,2048]{1,0:T(8,128)(2,1)}, bf16[3,512,512]{2,1,0:T(8,128)(2,1)}) custom-call(bf16[128,2048]{1,0:T(8,128)(2,1)} %get-tuple-element.110.refs_0_, bf16[128,2048]{1,0:T(8,128)(2,1)} %collective-permute-done.refs_1_, bf16[128,2048]{1,0:T(8,128)(2,1)} %collective-permute-done.1.refs_2_, bf16[128,2048]{1,0:T(8,128)(2,1)} %copy-done.13, ...), custom_call_target="tpu_custom_call" | custom-call | flops 322122560 | bytes 629145 | tf_op jit(solution)/shard_map/pallas_call | solution.py:189
  61.6 8.3 %collective-permute-done.6.refs_2_ = bf16[128,2048]{1,0:T(8,128)(2,1)S(1)} collective-permute-done((bf16[128,2048]{1,0:T(8,128)(2,1)S(1)}, bf16[128,2048]{1,0:T(8,128)(2,1)S(1)}, u32[]{:S(2)}, u32[]{:S(2)}) %collective-permute-start.6) | collective-permute-done | bytes 524320 | tf_op jit(solution)/shard_map/ppermute | solution.py:446
  80.3 17.7 %shard_map.214 = (bf16[512,2048]{1,0:T(8,128)(2,1)}, bf16[512,512]{1,0:T(8,128)(2,1)}, bf16[3,512,512]{2,1,0:T(8,128)(2,1)}, f32[3,1,512]{2,1,0:T(1,128)}) custom-call(bf16[128,2048]{1,0:T(8,128)(2,1)} %upstream.3, bf16[128,2048]{1,0:T(8,128)(2,1)} %copy-done.16, bf16[128,2048]{1,0:T(8,128)(2,1)} %copy-done.15, bf16[128,2048]{1,0:T(8,128)(2,1)} %copy-done.14, ...), custom_call_target="tpu_custom_call" | custom-call | flops 268435456 | bytes 524288 | tf_op jit(solution)/shard_map/pallas_call | solution.py:248
  98.0 3.9 %shard_map.216 = bf16[512,2048]{1,0:T(8,128)(2,1)} custom-call(s32[1]{0:T(128)} %constant.48.clone.1.place, bf16[512,512]{1,0:T(8,128)(2,1)} %get-tuple-element.151.refs_0_.context, bf16[512,2048]{1,0:T(8,128)(2,1)} %get-tuple-element.139.refs_1_.refs_5_), custom_call_target="tpu_custom_call" | custom-call | flops 107374184 | bytes 209715 | tf_op jit(solution)/shard_map/pallas_call | solution.py:389
  101.9 8.6 %shard_map.215 = bf16[3,2048,512]{2,1,0:T(8,128)(2,1)} custom-call(bf16[512,2048]{1,0:T(8,128)(2,1)} %get-tuple-element.132.left.refs_4_, bf16[3,512,512]{2,1,0:T(8,128)(2,1)} %get-tuple-element.153.right.part_grad), custom_call_target="tpu_custom_call" | custom-call | flops 322122560 | bytes 629145 | tf_op jit(solution)/shard_map/pallas_call | solution.py:278
  114.0 10.0 %collective-permute-done.11.refs_2_ = bf16[256,2048]{1,0:T(8,128)(2,1)} collective-permute-done((bf16[256,2048]{1,0:T(8,128)(2,1)S(1)}, bf16[256,2048]{1,0:T(8,128)(2,1)}, u32[]{:S(2)}, u32[]{:S(2)}) %collective-permute-start.11) | collective-permute-done | bytes 1048608 | tf_op jit(solution)/shard_map/ppermute | solution.py:446
  128.3 28.0 %shard_map.217 = (bf16[512,2048]{1,0:T(8,128)(2,1)}, bf16[512,2048]{1,0:T(8,128)(2,1)}, bf16[512,2048]{1,0:T(8,128)(2,1)}, bf16[512,2048]{1,0:T(8,128)(2,1)}, f3...) custom-call(bf16[256,2048]{1,0:T(8,128)(2,1)} %copy-done.1, ...), custom_call_target="tpu_custom_call" | custom-call | flops 1717986944 | bytes 3355443 | tf_op jit(solution)/shard_map/pallas_call | solution.py:323
  156.3 16.2 %collective-permute-done.16.refs_2_ = bf16[256,2048]{1,0:T(8,128)(2,1)S(1)} collective-permute-done((bf16[256,2048]{1,0:T(8,128)(2,1)S(1)}, bf16[256,2048]{1,0:T(8,128)(2,1)S(1)}, u32[]{:S(2)}, u32[]{:S(2)}) %collective-permute-start.16) | collective-permute-done | bytes 1048608 | tf_op jit(solution)/shard_map/ppermute | solution.py:446
  176.2 14.9 %shard_map.219 = (bf16[512,2048]{1,0:T(8,128)(2,1)}, bf16[512,2048]{1,0:T(8,128)(2,1)}, bf16[512,2048]{1,0:T(8,128)(2,1)}, bf16[512,2048]{1,0:T(8,128)(2,1)}, f32[1,2048]{1,0:T(1,128)}) custom-call(bf16[256,2048]{1,0:T(8,128)(2,1)} %copy-done.2, bf16[256,2048]{1,0:T(8,128)(2,1)} %copy-done.9, bf16[256,2048]{1,0:T(8,128)(2,1)} %copy-done.7, ...), custom_call_target="tpu_custom_call" | custom-call | flops 858993472 | bytes 1677721 | tf_op jit(solution)/shard_map/pallas_call | solution.py:323
  191.0 19.8 %shard_map.218 = (f32[256,2048]{1,0:T(8,128)}, bf16[256,2048]{1,0:T(8,128)(2,1)}, bf16[256,2048]{1,0:T(8,128)(2,1)}, bf16[256,2048]{1,0:T(8,128)(2,1)}) custom-call(bf16[512,2048]{1,0:T(8,128)(2,1)} %get-tuple-element.150.active.refs_0_, bf16[512,512]{1,0:T(8,128)(2,1)} %get-tuple-element.151.refs_0_.context, ...), custom_call_target="tpu_custom_call" | custom-call | flops 1288490240 | bytes 2516582 | tf_op jit(solution)/shard_map/pallas_call | solution.py:357
  210.9 10.2 %collective-permute-done.19.refs_2_ = bf16[256,2048]{1,0:T(8,128)(2,1)S(1)} collective-permute-done((bf16[256,2048]{1,0:T(8,128)(2,1)S(1)}, bf16[256,2048]{1,0:T(8,128)(2,1)S(1)}, u32[]{:S(2)}, u32[]{:S(2)}) %collective-permute-start.19) | collective-permute-done | bytes 1048608 | tf_op jit(solution)/shard_map/ppermute | solution.py:446
  224.8 15.2 %shard_map.220 = (bf16[512,2048]{1,0:T(8,128)(2,1)}, bf16[512,2048]{1,0:T(8,128)(2,1)}, bf16[512,2048]{1,0:T(8,128)(2,1)}, bf16[512,2048]{1,0:T(8,128)(2,1)}, f32[1,2048]{1,0:T(1,128)}) custom-call(bf16[256,2048]{1,0:T(8,128)(2,1)} %copy-done.3, bf16[256,2048]{1,0:T(8,128)(2,1)} %copy-done.10, bf16[256,2048]{1,0:T(8,128)(2,1)} %copy-done.8, ...), custom_call_target="tpu_custom_call" | custom-call | flops 858993472 | bytes 1677721 | tf_op jit(solution)/shard_map/pallas_call | solution.py:323
  239.9 24.1 %shard_map.226.refs_0_ = bf16[2048,2048]{1,0:T(8,128)(2,1)} custom-call(s32[1]{0:T(128)} %bitcast.13.place, bf16[512,2048]{1,0:T(8,128)(2,1)} %get-tuple-element.150.active.refs_0_, bf16[512,2048]{1,0:T(8,128)(2,1)} %get-tuple-element.192.refs_1_, bf16[512,2048]{1,0:T(8,128)(2,1)} %get-tuple-element.193.refs_2_, ...), custom_call_target="tpu_custom_call" | custom-call | flops 1717986944 | bytes 3355443 | tf_op jit(solution)/shard_map/pallas_call | solution.py:389
  264.1 24.4 %shard_map.221.refs_0_ = bf16[2048,2048]{1,0:T(8,128)(2,1)} custom-call(s32[1]{0:T(128)} %bitcast.13.place, bf16[512,2048]{1,0:T(8,128)(2,1)} %get-tuple-element.168.refs_0_, bf16[512,2048]{1,0:T(8,128)(2,1)} %get-tuple-element.169.refs_1_, bf16[512,2048]{1,0:T(8,128)(2,1)} %get-tuple-element.170.refs_2_, bf16[512,2048]{1,0:T(8,128)(2,1)} %get-tuple-element.175.refs_3_, ...), custom_call_target="tpu_custom_call" | custom-call | flops 1717986944 | bytes 3355443 | tf_op jit(solution)/shard_map/pallas_call | solution.py:389
  288.5 17.0 %all-reduce.3.cloned.1.call-done = (bf16[3,2048,512]{2,1,0:T(8,128)(2,1)}, bf16[512,2048]{1,0:T(8,128)(2,1)}) async-done(((bf16[3,2048,512]{2,1,0:T(8,128)(2,1)}, bf16[512,2048]{1,0:T(8,128)(2,1)}), (bf16[3,2048,512]{2,1,0:T(8,128)(2,1)}, bf16[512,2048]{1,0:T(8,128)(2,1)})) %all-reduce.3.cloned.1.call-update) | async-done | bytes 8388624 | tf_op jit(solution)/shard_map/psum | solution.py:502
  305.5 5.4 %shard_map.222 = (bf16[128,2048]{1,0:T(8,128)(2,1)}, f32[128,2048]{1,0:T(8,128)}, f32[3,2048]{1,0:T(4,128)}) custom-call(bf16[128,2048]{1,0:T(8,128)(2,1)} %tokens.3, bf16[128,2048]{1,0:T(8,128)(2,1)} %upstream.3, f32[1,2048]{1,0:T(1,128)} %bitcast.38, f32[1,2048]{1,0:T(1,128)} %bitcast.46, f32[256,2048]{1,0:T(8,128)} %get-tuple-element.180.own, ...), custom_call_target="tpu_custom_call" | custom-call | flops 26843544 | bytes 52428 | tf_op jit(solution)/shard_map/pallas_call | solution.py:153
  327.8 3.9 %shard_map.224 = f32[512,2048]{1,0:T(8,128)} custom-call(bf16[512,2048]{1,0:T(8,128)(2,1)} %get-tuple-element.190.refs_0_), custom_call_target="tpu_custom_call" | custom-call | flops 26843544 | bytes 52428 | tf_op jit(solution)/shard_map/pallas_call | solution.py:413
  331.7 7.4 %shard_map.223 = f32[6144,512]{1,0:T(8,128)} custom-call(bf16[6144,512]{1,0:T(8,128)(2,1)} %bitcast.34), custom_call_target="tpu_custom_call" | custom-call | flops 80530640 | bytes 157286 | tf_op jit(solution)/shard_map/pallas_call | solution.py:413
  340.4 11.7 %shard_map.227 = f32[2048,2048]{1,0:T(8,128)} custom-call(bf16[2048,2048]{1,0:T(8,128)(2,1)} %shard_map.226.refs_0_, bf16[2048,2048]{1,0:T(8,128)(2,1)} %collective-permute-done.30.refs_1_), custom_call_target="tpu_custom_call" | custom-call | flops 107374184 | bytes 209715 | tf_op jit(solution)/shard_map/pallas_call | solution.py:413
  352.1 11.7 %shard_map.225 = f32[2048,2048]{1,0:T(8,128)} custom-call(bf16[2048,2048]{1,0:T(8,128)(2,1)} %shard_map.221.refs_0_, bf16[2048,2048]{1,0:T(8,128)(2,1)} %collective-permute-done.29.refs_1_), custom_call_target="tpu_custom_call" | custom-call | flops 107374184 | bytes 209715 | tf_op jit(solution)/shard_map/pallas_call | solution.py:413
  (133 shorter events, 65.4 us)
Async XLA Ops:
  7.2 298.3 %all-reduce.3.cloned.1.call-start = ((), (), s32[]{:S(2)}) async-start(), calls=%async_computation | async-start | bytes 16777216 | tf_op jit(solution)/shard_map/psum | solution.py:502
  13.9 23.5 %collective-permute-start.1 = (bf16[128,2048]{1,0:T(8,128)(2,1)}, bf16[128,2048]{1,0:T(8,128)(2,1)}, u32[]{:S(2)}, u32[]{:S(2)}) collective-permute-start(bf16[128,2048]{1,0:T(8,128)(2,1)} %get-tuple-element.110.refs_0_), channel_id=1, source_target_pairs={{0,2},{1,3},{2,0},{3,1},{4,6},{5,7},{6,4},{7,5},{8,10},{9,11},{10,... | collective-permute-start | bytes 1572872 | tf_op jit(solution)/shard_map/ppermute | solution.py:446
  14.4 23.3 %collective-permute-start = (bf16[128,2048]{1,0:T(8,128)(2,1)}, bf16[128,2048]{1,0:T(8,128)(2,1)}, u32[]{:S(2)}, u32[]{:S(2)}) collective-permute-start(bf16[128,2048]{1,0:T(8,128)(2,1)} %get-tuple-element.110.refs_0_), channel_id=1, source_target_pairs={{0,1},{1,0},{2,3},{3,2},{4,5},{5,4},{6,7},{7,6},{8,9},{9,8},{10,11... | collective-permute-start | bytes 1572872 | tf_op jit(solution)/shard_map/ppermute | solution.py:446
  14.5 26.5 %collective-permute-start.4 = (bf16[256,2048]{1,0:T(8,128)(2,1)}, bf16[256,2048]{1,0:T(8,128)(2,1)S(1)}, u32[]{:S(2)}, u32[]{:S(2)}) collective-permute-start(bf16[256,2048]{1,0:T(8,128)(2,1)} %get-tuple-element.106), channel_id=1, source_target_pairs={{8,0},{12,4},{16,8},{20,12},{24,16},{28,20},{9,1},{13,5},{17,9},{2... | collective-permute-start | bytes 3145736 | tf_op jit(solution)/shard_map/ppermute | solution.py:455
  15.8 26.5 %collective-permute-start.3 = (bf16[256,2048]{1,0:T(8,128)(2,1)}, bf16[256,2048]{1,0:T(8,128)(2,1)}, u32[]{:S(2)}, u32[]{:S(2)}) collective-permute-start(bf16[256,2048]{1,0:T(8,128)(2,1)} %get-tuple-element.106), channel_id=1, source_target_pairs={{0,8},{4,12},{8,16},{12,20},{16,24},{20,28},{1,9},{5,13},{9,17},{1... | collective-permute-start | bytes 3145736 | tf_op jit(solution)/shard_map/ppermute | solution.py:455
  42.2 27.6 %collective-permute-start.8 = (bf16[256,2048]{1,0:T(8,128)(2,1)}, bf16[256,2048]{1,0:T(8,128)(2,1)}, u32[]{:S(2)}, u32[]{:S(2)}) collective-permute-start(bf16[256,2048]{1,0:T(8,128)(2,1)} %collective-permute-done.3), channel_id=1, source_target_pairs={{8,16},{12,20},{16,24},{20,28},{9,17},{13,21},{17,25},{21,29},{10,... | collective-permute-start | bytes 3145736 | tf_op jit(solution)/shard_map/ppermute | solution.py:455
  43.9 28.3 %collective-permute-start.9 = (bf16[256,2048]{1,0:T(8,128)(2,1)S(1)}, bf16[256,2048]{1,0:T(8,128)(2,1)}, u32[]{:S(2)}, u32[]{:S(2)}) collective-permute-start(bf16[256,2048]{1,0:T(8,128)(2,1)S(1)} %collective-permute-done.4), channel_id=1, source_target_pairs={{8,0},{12,4},{16,8},{20,12},{9,1},{13,5},{17,9},{21,13},{10,2},{14... | collective-permute-start | bytes 3145736 | tf_op jit(solution)/shard_map/ppermute | solution.py:455
  48.4 21.4 %collective-permute-start.6 = (bf16[128,2048]{1,0:T(8,128)(2,1)S(1)}, bf16[128,2048]{1,0:T(8,128)(2,1)S(1)}, u32[]{:S(2)}, u32[]{:S(2)}) collective-permute-start(bf16[128,2048]{1,0:T(8,128)(2,1)S(1)} %copy-done), channel_id=1, source_target_pairs={{0,2},{1,3},{2,0},{3,1},{4,6},{5,7},{6,4},{7,5},{8,10},{9,11},{10,... | collective-permute-start | bytes 1572872 | tf_op jit(solution)/shard_map/ppermute | solution.py:446
  72.2 39.7 %collective-permute-start.14 = (bf16[256,2048]{1,0:T(8,128)(2,1)}, bf16[256,2048]{1,0:T(8,128)(2,1)}, u32[]{:S(2)}, u32[]{:S(2)}) collective-permute-start(bf16[256,2048]{1,0:T(8,128)(2,1)} %collective-permute-done.8), channel_id=1, source_target_pairs={{16,24},{20,28},{17,25},{21,29},{18,26},{22,30},{19,27},{23,31}} | collective-permute-start | bytes 3145736 | tf_op jit(solution)/shard_map/ppermute | solution.py:455
  73.8 38.1 %collective-permute-start.13 = (bf16[256,2048]{1,0:T(8,128)(2,1)}, bf16[256,2048]{1,0:T(8,128)(2,1)}, u32[]{:S(2)}, u32[]{:S(2)}) collective-permute-start(bf16[256,2048]{1,0:T(8,128)(2,1)} %collective-permute-done.9), channel_id=1, source_target_pairs={{8,0},{12,4},{9,1},{13,5},{10,2},{14,6},{11,3},{15,7}} | collective-permute-start | bytes 3145736 | tf_op jit(solution)/shard_map/ppermute | solution.py:455
  76.8 37.2 %collective-permute-start.12 = (bf16[256,2048]{1,0:T(8,128)(2,1)S(1)}, bf16[256,2048]{1,0:T(8,128)(2,1)}, u32[]{:S(2)}, u32[]{:S(2)}) collective-permute-start(bf16[256,2048]{1,0:T(8,128)(2,1)S(1)} %broadcast_select_fusion.1.refs_0_), channel_id=1, source_target_pairs={{0,3},{1,2},{2,1},{3,0},{4,7},{5,6},{6,5},{7,4},{8,11},{9,10},{10,... | collective-permute-start | bytes 3145736 | tf_op jit(solution)/shard_map/ppermute | solution.py:446
  79.3 44.8 %collective-permute-start.11 = (bf16[256,2048]{1,0:T(8,128)(2,1)S(1)}, bf16[256,2048]{1,0:T(8,128)(2,1)}, u32[]{:S(2)}, u32[]{:S(2)}) collective-permute-start(bf16[256,2048]{1,0:T(8,128)(2,1)S(1)} %broadcast_select_fusion.1.refs_0_), channel_id=1, source_target_pairs={{0,2},{1,3},{2,0},{3,1},{4,6},{5,7},{6,4},{7,5},{8,10},{9,11},{10,... | collective-permute-start | bytes 3145736 | tf_op jit(solution)/shard_map/ppermute | solution.py:446
  79.8 44.3 %collective-permute-start.10 = (bf16[256,2048]{1,0:T(8,128)(2,1)S(1)}, bf16[256,2048]{1,0:T(8,128)(2,1)}, u32[]{:S(2)}, u32[]{:S(2)}) collective-permute-start(bf16[256,2048]{1,0:T(8,128)(2,1)S(1)} %broadcast_select_fusion.1.refs_0_), channel_id=1, source_target_pairs={{0,1},{1,0},{2,3},{3,2},{4,5},{5,4},{6,7},{7,6},{8,9},{9,8},{10,11... | collective-permute-start | bytes 3145736 | tf_op jit(solution)/shard_map/ppermute | solution.py:446
  124.1 32.2 %collective-permute-start.17 = (bf16[256,2048]{1,0:T(8,128)(2,1)S(1)}, bf16[256,2048]{1,0:T(8,128)(2,1)S(1)}, u32[]{:S(2)}, u32[]{:S(2)}) collective-permute-start(bf16[256,2048]{1,0:T(8,128)(2,1)S(1)} %broadcast_select_fusion.refs_0_), channel_id=1, source_target_pairs={{0,3},{1,2},{2,1},{3,0},{4,7},{5,6},{6,5},{7,4},{8,11},{9,10},{10,... | collective-permute-start | bytes 3145736 | tf_op jit(solution)/shard_map/ppermute | solution.py:446
  125.6 46.9 %collective-permute-start.16 = (bf16[256,2048]{1,0:T(8,128)(2,1)S(1)}, bf16[256,2048]{1,0:T(8,128)(2,1)S(1)}, u32[]{:S(2)}, u32[]{:S(2)}) collective-permute-start(bf16[256,2048]{1,0:T(8,128)(2,1)S(1)} %broadcast_select_fusion.refs_0_), channel_id=1, source_target_pairs={{0,2},{1,3},{2,0},{3,1},{4,6},{5,7},{6,4},{7,5},{8,10},{9,11},{10,... | collective-permute-start | bytes 3145736 | tf_op jit(solution)/shard_map/ppermute | solution.py:446
  127.1 45.6 %collective-permute-start.15 = (bf16[256,2048]{1,0:T(8,128)(2,1)S(1)}, bf16[256,2048]{1,0:T(8,128)(2,1)S(1)}, u32[]{:S(2)}, u32[]{:S(2)}) collective-permute-start(bf16[256,2048]{1,0:T(8,128)(2,1)S(1)} %broadcast_select_fusion.refs_0_), channel_id=1, source_target_pairs={{0,1},{1,0},{2,3},{3,2},{4,5},{5,4},{6,7},{7,6},{8,9},{9,8},{10,11... | collective-permute-start | bytes 3145736 | tf_op jit(solution)/shard_map/ppermute | solution.py:446
  172.7 38.2 %collective-permute-start.20 = (bf16[256,2048]{1,0:T(8,128)(2,1)S(1)}, bf16[256,2048]{1,0:T(8,128)(2,1)S(1)}, u32[]{:S(2)}, u32[]{:S(2)}) collective-permute-start(bf16[256,2048]{1,0:T(8,128)(2,1)S(1)} %select_select_fusion.refs_0_), channel_id=1, source_target_pairs={{0,3},{1,2},{2,1},{3,0},{4,7},{5,6},{6,5},{7,4},{8,11},{9,10},{10,... | collective-permute-start | bytes 3145736 | tf_op jit(solution)/shard_map/ppermute | solution.py:446
  174.1 47.0 %collective-permute-start.19 = (bf16[256,2048]{1,0:T(8,128)(2,1)S(1)}, bf16[256,2048]{1,0:T(8,128)(2,1)S(1)}, u32[]{:S(2)}, u32[]{:S(2)}) collective-permute-start(bf16[256,2048]{1,0:T(8,128)(2,1)S(1)} %select_select_fusion.refs_0_), channel_id=1, source_target_pairs={{0,2},{1,3},{2,0},{3,1},{4,6},{5,7},{6,4},{7,5},{8,10},{9,11},{10,... | collective-permute-start | bytes 3145736 | tf_op jit(solution)/shard_map/ppermute | solution.py:446
  175.6 45.7 %collective-permute-start.18 = (bf16[256,2048]{1,0:T(8,128)(2,1)S(1)}, bf16[256,2048]{1,0:T(8,128)(2,1)S(1)}, u32[]{:S(2)}, u32[]{:S(2)}) collective-permute-start(bf16[256,2048]{1,0:T(8,128)(2,1)S(1)} %select_select_fusion.refs_0_), channel_id=1, source_target_pairs={{0,1},{1,0},{2,3},{3,2},{4,5},{5,4},{6,7},{7,6},{8,9},{9,8},{10,11... | collective-permute-start | bytes 3145736 | tf_op jit(solution)/shard_map/ppermute | solution.py:446
  221.3 67.2 %collective-permute-start.21 = (bf16[256,2048]{1,0:T(8,128)(2,1)}, bf16[256,2048]{1,0:T(8,128)(2,1)S(1)}, u32[]{:S(2)}, u32[]{:S(2)}) collective-permute-start(bf16[256,2048]{1,0:T(8,128)(2,1)} %get-tuple-element.165), channel_id=1, source_target_pairs={{0,1},{1,0},{2,3},{3,2},{4,5},{5,4},{6,7},{7,6},{8,9},{9,8},{10,11... | collective-permute-start | bytes 3145736 | tf_op jit(solution)/shard_map/ppermute | solution.py:446
  222.7 65.7 %collective-permute-start.22 = (bf16[256,2048]{1,0:T(8,128)(2,1)}, bf16[256,2048]{1,0:T(8,128)(2,1)S(1)}, u32[]{:S(2)}, u32[]{:S(2)}) collective-permute-start(bf16[256,2048]{1,0:T(8,128)(2,1)} %get-tuple-element.166), channel_id=1, source_target_pairs={{0,2},{1,3},{2,0},{3,1},{4,6},{5,7},{6,4},{7,5},{8,10},{9,11},{10,... | collective-permute-start | bytes 3145736 | tf_op jit(solution)/shard_map/ppermute | solution.py:446
  223.3 65.2 %collective-permute-start.23 = (bf16[256,2048]{1,0:T(8,128)(2,1)}, bf16[256,2048]{1,0:T(8,128)(2,1)}, u32[]{:S(2)}, u32[]{:S(2)}) collective-permute-start(bf16[256,2048]{1,0:T(8,128)(2,1)} %get-tuple-element.167), channel_id=1, source_target_pairs={{0,3},{1,2},{2,1},{3,0},{4,7},{5,6},{6,5},{7,4},{8,11},{9,10},{10,... | collective-permute-start | bytes 3145736 | tf_op jit(solution)/shard_map/ppermute | solution.py:446
  264.1 76.3 %collective-permute-start.30 = (bf16[2048,2048]{1,0:T(8,128)(2,1)}, bf16[2048,2048]{1,0:T(8,128)(2,1)}, u32[]{:S(2)}, u32[]{:S(2)}) collective-permute-start(bf16[2048,2048]{1,0:T(8,128)(2,1)} %shard_map.226.refs_0_), channel_id=1, source_target_pairs={{0,4},{4,0},{8,12},{12,8},{16,20},{20,16},{24,28},{28,24},{1,5},{5... | collective-permute-start | bytes 25165832 | tf_op jit(solution)/shard_map/ppermute | solution.py:449
  305.5 46.6 %collective-permute-start.29 = (bf16[2048,2048]{1,0:T(8,128)(2,1)}, bf16[2048,2048]{1,0:T(8,128)(2,1)}, u32[]{:S(2)}, u32[]{:S(2)}) collective-permute-start(bf16[2048,2048]{1,0:T(8,128)(2,1)} %shard_map.221.refs_0_), channel_id=1, source_target_pairs={{0,4},{4,0},{8,12},{12,8},{16,20},{20,16},{24,28},{28,24},{1,5},{5... | collective-permute-start | bytes 25165832 | tf_op jit(solution)/shard_map/ppermute | solution.py:449
  (31 other events, 551.0 us)
Sparse Core Ops, SparseCore 0:
  124.3 181.2 all-reduce.2
